TPU v7x, 256 devices: a whole 4x4x8 slice. The times are simulated.
256 devices in a mesh: shot: 8 (over z_hi, y), pencil: 32 (over z_lo, x, core).
Axes of the slice: x: 4, y: 4, z: 8 (z_hi: 2, z_lo: 4; z = z_hi * 4 + z_lo), core: 2. Of those that a mesh axis runs over, the one named last changes fastest.
Arguments:
- contrast_source: float32 [16, 2, 256, 256, 128], P('shot', None, 'pencil'), may hold values from -6 to 6
- green_spectrum: float32 [2, 256, 256, 128], P(None, None, 'pencil'), may hold values from -4 to 4
- source_cells: int32 [16, 3], P('shot'), may hold values from 0 to 127
Outputs:
- updated_source: float32 [16, 2, 256, 256, 128], P('shot', None, 'pencil')
- contrast: float32 [2, 256, 256, 128], P(None, 'pencil', 'shot')
Inputs may be any that keep to these rules, and one draw needn't show every extreme that they name: `source_cells`: each row is one source's cell (x, y, z).
All inputs are finite; a program needn't handle non-finite values.
Results may differ from a plain program's by a relative error of at most 0.0003.
Values sent between devices are 32-bit elements; how exact they have to be, the bound alone decides.
No kernel may reach another device: no remote copies, remote signals or barrier semaphores. Data moves between devices by JAX's collectives and lax.ppermute only.
A program may use at most 64 MiB of HBM per device.

v0:
```python
import math

import jax
import jax.numpy as jnp
from jax import lax
from jax.sharding import PartitionSpec as P


def dft_table(length, sign):
    grid_index = jnp.arange(length, dtype=jnp.int32)
    product = grid_index[:, None] * grid_index[None, :] % length
    angle = 2.0 * math.pi / length * product.astype(jnp.float32)
    cosine = jnp.cos(angle) / math.sqrt(length)
    sine = sign * jnp.sin(angle) / math.sqrt(length)
    return jnp.stack([jnp.stack([cosine, -sine]), jnp.stack([sine, cosine])])


def along_z(values, matrix):
    return jnp.einsum("scxyj,cdjk->sdxyk", values, matrix, precision=lax.Precision.HIGHEST)


def along_y(values, matrix):
    return jnp.einsum("scxjz,cdjk->sdxkz", values, matrix, precision=lax.Precision.HIGHEST)


def along_x(values, matrix):
    return jnp.einsum("scjyz,cdjk->sdkyz", values, matrix, precision=lax.Precision.HIGHEST)


def solve_fields(sources, cells, green_local, forward_move, back_move):
    count_y = sources.shape[3]
    count_z = sources.shape[4]
    count_x = green_local.shape[1]
    spectra = along_y(along_z(sources, dft_table(count_z, 1.0)), dft_table(count_y, 1.0))
    forward_x = dft_table(count_x, 1.0)

    def transform_x(values):
        return along_x(values, forward_x)

    spectra = forward_move(spectra, transform_x)
    part_y = spectra.shape[3]
    wave_x = jnp.arange(count_x, dtype=jnp.int32)[None, :, None, None]
    wave_y = (lax.axis_index("pencil") * part_y + jnp.arange(part_y, dtype=jnp.int32))[
        None, None, :, None
    ]
    wave_z = jnp.arange(count_z, dtype=jnp.int32)[None, None, None, :]
    cell_x = cells[:, 0][:, None, None, None]
    cell_y = cells[:, 1][:, None, None, None]
    cell_z = cells[:, 2][:, None, None, None]
    turns = (wave_x * cell_x % count_x).astype(jnp.float32) / count_x
    turns = turns + (wave_y * cell_y % count_y).astype(jnp.float32) / count_y
    turns = turns + (wave_z * cell_z % count_z).astype(jnp.float32) / count_z
    angle = 2.0 * math.pi * turns
    front_re = spectra[:, 0] + jnp.cos(angle)
    front_im = spectra[:, 1] - jnp.sin(angle)
    image = jnp.stack(
        [
            green_local[0] * front_re - green_local[1] * front_im,
            green_local[0] * front_im + green_local[1] * front_re,
        ],
        axis=1,
    )
    image = along_x(image, dft_table(count_x, -1.0))
    fields = back_move(image)
    return along_z(along_y(fields, dft_table(count_y, -1.0)), dft_table(count_z, -1.0))


def shards(contrast_source, green_spectrum, source_cells):
    group = contrast_source.shape[0]

    def forward_one(values, transform):
        return transform(lax.all_to_all(values, "pencil", split_axis=3, concat_axis=2, tiled=True))

    def back_one(values):
        return lax.all_to_all(values, "pencil", split_axis=2, concat_axis=3, tiled=True)

    fields = jnp.concatenate(
        [
            solve_fields(
                contrast_source[member : member + 1],
                source_cells[member : member + 1],
                green_spectrum,
                forward_one,
                back_one,
            )
            for member in range(group)
        ],
        axis=0,
    )
    field_re = fields[:, 0]
    field_im = fields[:, 1]
    source_re = contrast_source[:, 0]
    source_im = contrast_source[:, 1]
    numerator = jnp.stack(
        [
            jnp.sum(field_re * source_re + field_im * source_im, axis=0),
            jnp.sum(field_re * source_im - field_im * source_re, axis=0),
        ]
    )
    weight = jnp.sum(field_re * field_re + field_im * field_im, axis=0)
    numer_all, weight_all = lax.psum((numerator, weight), "shot")
    contrast = numer_all / (1.0 + weight_all)[None]
    share_rows = contrast.shape[2] // lax.axis_size("shot")
    contrast_share = lax.dynamic_slice_in_dim(
        contrast, lax.axis_index("shot") * share_rows, share_rows, 2
    )
    scattered = jnp.stack(
        [
            contrast[0] * field_re - contrast[1] * field_im,
            contrast[0] * field_im + contrast[1] * field_re,
        ],
        axis=1,
    )
    updated = 0.5 * (contrast_source + scattered)
    return (updated, contrast_share)


def solution(mesh):
    return jax.shard_map(
        shards,
        mesh=mesh,
        in_specs=(
            P("shot", None, "pencil", None, None),
            P(None, None, "pencil", None),
            P("shot", None),
        ),
        out_specs=(P("shot", None, "pencil", None, None), P(None, "pencil", "shot", None)),
        check_vma=False,
    )
```

profile of v0, /device:TPU:1, one launch (start us, length us, event | category | flops | bytes accessed | tf_op | source)
XLA Modules:
  0.0 471.4 jit_solution(4426242499651342878)
XLA Ops:
  11.0 3.9 fusion.127
  17.1 3.6 fusion.38
  23.3 10.1 %all-to-all-start = ((f32[1,2,8,256,128]{4,2,1,0,3:T(8,128)}), f32[1,2,8,256,128]{4,2,1,0,3:T(8,128)}, u32[]{:S(2)}, u32[]{:S(2)}) async-start(f32[1,2,8,256,128]{4,2,1,0,3:T(8,128)} %copy.38), calls=%async_computation | async-start | bytes 4194304 | tf_op jit(solution)/shard_map/all_to_all | solution.py:72
  33.4 3.5 fusion.2
  36.9 3.6 fusion.47
  43.0 38.5 %all-to-all-done = f32[1,2,8,256,128]{4,2,1,0,3:T(8,128)} async-done(((f32[1,2,8,256,128]{4,2,1,0,3:T(8,128)}), f32[1,2,8,256,128]{4,2,1,0,3:T(8,128)}, u32[]{:S(2)}, u32[]{:S(2)}) %all-to-all-start) | async-done | bytes 2097184 | tf_op jit(solution)/shard_map/all_to_all | solution.py:72
  81.6 7.0 %all-to-all-start.2 = ((f32[1,2,8,256,128]{4,2,1,0,3:T(8,128)}), f32[1,2,8,256,128]{4,2,1,0,3:T(8,128)}, u32[]{:S(2)}, u32[]{:S(2)}) async-start(f32[1,2,8,256,128]{4,2,1,0,3:T(8,128)} %copy.50), calls=%async_computation.2 | async-start | bytes 4194304 | tf_op jit(solution)/shard_map/all_to_all | solution.py:72
  96.0 6.5 %fusion.41 = f32[1,2,256,8,128]{4,2,3,1,0:T(8,128)} fusion(f32[1,2,8,32,8,128]{5,2,1,4,3,0:T(8,128)} %bitcast.30, f32[1,2,256,256]{2,3,0,1:T(8,128)S(1)} %get-tuple-element.28, f32[1,2,256,256]{2,3,0,1:T(8,128)S(1)} %get-tuple-element.29), kind=kOutput, calls=%fused_computation.49 | convolution fusion | flops 3221487616 | bytes 5242880 | tf_op jit(solution)/shard_map/scjyz,cdjk->sdkyz/dot_general | solution.py:27
  102.5 34.1 %all-to-all-done.2 = f32[1,2,8,256,128]{4,2,1,0,3:T(8,128)} async-done(((f32[1,2,8,256,128]{4,2,1,0,3:T(8,128)}), f32[1,2,8,256,128]{4,2,1,0,3:T(8,128)}, u32[]{:S(2)}, u32[]{:S(2)}) %all-to-all-start.2) | async-done | bytes 2097184 | tf_op jit(solution)/shard_map/all_to_all | solution.py:72
  136.6 5.3 %fusion.50 = f32[1,2,256,8,128]{4,2,3,1,0:T(8,128)S(1)} fusion(f32[1,2,8,32,8,128]{5,2,1,4,3,0:T(8,128)} %bitcast.79, f32[1,2,256,256]{2,3,0,1:T(8,128)S(1)} %get-tuple-element.28, f32[1,2,256,256]{2,3,0,1:T(8,128)S(1)} %get-tuple-element.29), kind=kOutput, calls=%fused_computation.52 | convolution fusion | flops 3221487616 | bytes 5242880 | tf_op jit(solution)/shard_map/scjyz,cdjk->sdkyz/dot_general | solution.py:27
  141.9 9.0 %subtract_bitcast_fusion.1 = (f32[1,1,256,8,128]{4,2,3,1,0:T(8,128)S(1)}, f32[1,1,256,8,128]{4,2,3,1,0:T(8,128)S(1)}, f32[1,1,256,8,128]{4,2,3,1,0:T(8,128)}, f32[1,1,256,8,128]{4,2,3,1,0:T(8,128)}) fusion(f32[1,256,8,128]{3,2,1,0:T(8,128)S(1)} %copy-done.4, f32[1,256,8,128]{3,2,1,0:T(8,128)S(1)} %get-tuple-element.25, ...), kind=kLoop, calls=%fused_computation.77 | loop fusion | flops 5242880 | bytes 10503168 | tf_op jit(solution)/shard_map/stack | solution.py:56
  150.9 3.6 fusion.32
  157.0 6.4 %all-to-all-start.1 = ((f32[1,2,256,8,128]{4,3,1,0,2:T(8,128)}), f32[1,2,256,8,128]{4,3,1,0,2:T(8,128)S(1)}, u32[]{:S(2)}, u32[]{:S(2)}) async-start(f32[1,2,256,8,128]{4,3,1,0,2:T(8,128)} %copy.43), calls=%async_computation.1 | async-start | bytes 4194304 | tf_op jit(solution)/shard_map/all_to_all | solution.py:75
  163.3 5.1 %fusion.35 = f32[1,2,256,8,128]{4,2,3,1,0:T(8,128)S(1)} fusion(f32[1,1,256,8,128]{4,2,3,1,0:T(8,128)} %get-tuple-element.23, f32[1,1,256,8,128]{4,2,3,1,0:T(8,128)} %get-tuple-element.24, f32[1,2,256,256]{2,3,1,0:T(8,128)S(1)} %get-tuple-element.30, f32[1,2,256,256]{2,3,1,0:T(8,128)S(1)} %get-tuple-element.27), kind=kOutput, calls=%fused_computation.47 | convolution fusion | flops 3222011904 | bytes 5242880 | tf_op jit(solution)/shard_map/scjyz,cdjk->sdkyz/dot_general | solution.py:27
  171.0 40.5 %all-to-all-done.1 = f32[1,2,256,8,128]{4,3,1,0,2:T(8,128)S(1)} async-done(((f32[1,2,256,8,128]{4,3,1,0,2:T(8,128)}), f32[1,2,256,8,128]{4,3,1,0,2:T(8,128)S(1)}, u32[]{:S(2)}, u32[]{:S(2)}) %all-to-all-start.1) | async-done | bytes 2097184 | tf_op jit(solution)/shard_map/all_to_all | solution.py:75
  211.5 6.4 %all-to-all-start.3 = ((f32[1,2,256,8,128]{4,3,1,0,2:T(8,128)}), f32[1,2,256,8,128]{4,3,1,0,2:T(8,128)}, u32[]{:S(2)}, u32[]{:S(2)}) async-start(f32[1,2,256,8,128]{4,3,1,0,2:T(8,128)} %copy.54), calls=%async_computation.3 | async-start | bytes 4194304 | tf_op jit(solution)/shard_map/all_to_all | solution.py:75
  217.9 5.4 %copy.61 = f32[2,2,8,256,128]{3,4,2,1,0:T(8,128)} copy(f32[2,2,8,256,128]{4,3,2,1,0:T(8,128)} %param.3) | data formatting | bytes 8388608 | tf_op args[0]
  223.3 4.9 %fusion.44 = f32[2,8,256,128]{3,2,1,0:T(8,128)} fusion(f32[1,2,32,8,8,128]{5,4,1,3,2,0:T(8,128)S(1)} %bitcast.274, f32[1,2,256,256]{2,3,1,0:T(8,128)S(1)} %get-tuple-element.30, f32[1,2,256,256]{2,3,1,0:T(8,128)S(1)} %get-tuple-element.27), kind=kOutput, calls=%fused_computation.50 | convolution fusion | flops 3221487616 | bytes 5242880 | tf_op jit(solution)/shard_map/scxjz,cdjk->sdxkz/dot_general | solution.py:23
  228.2 37.9 %all-to-all-done.3 = f32[1,2,256,8,128]{4,3,1,0,2:T(8,128)} async-done(((f32[1,2,256,8,128]{4,3,1,0,2:T(8,128)}), f32[1,2,256,8,128]{4,3,1,0,2:T(8,128)}, u32[]{:S(2)}, u32[]{:S(2)}) %all-to-all-start.3) | async-done | bytes 2097184 | tf_op jit(solution)/shard_map/all_to_all | solution.py:75
  266.1 5.3 %fusion.53 = f32[2,8,256,128]{3,2,1,0:T(8,128)S(1)} fusion(f32[1,2,32,8,8,128]{5,4,1,3,2,0:T(8,128)} %bitcast.98, f32[1,2,256,256]{2,3,1,0:T(8,128)S(1)} %get-tuple-element.30, f32[1,2,256,256]{2,3,1,0:T(8,128)S(1)} %get-tuple-element.27), kind=kOutput, calls=%fused_computation.53 | convolution fusion | flops 3221487616 | bytes 5242880 | tf_op jit(solution)/shard_map/scxjz,cdjk->sdxkz/dot_general | solution.py:23
  275.6 3.7 add_reduce_fusion.1
  280.8 166.9 %all-reduce.3.cloned.1.call-done = (f32[2,8,256,128]{2,3,1,0:T(8,128)}, f32[8,256,128]{1,2,0:T(8,128)}) async-done(((f32[2,8,256,128]{2,3,1,0:T(8,128)}, f32[8,256,128]{1,2,0:T(8,128)}), (f32[2,8,256,128]{2,3,1,0:T(8,128)}, f32[8,256,128]{1,2,0:T(8,128)})) %all-reduce.3.cloned.1.call-update) | async-done | bytes 3145744 | tf_op jit(solution)/shard_map/psum | solution.py:101
  452.8 2.9 multiply_subtract_fusion
  458.9 5.3 %copy.62 = f32[2,2,8,256,128]{4,3,2,1,0:T(8,128)} copy(f32[2,2,8,256,128]{3,4,2,1,0:T(8,128)} %fusion) | data formatting | bytes 8388608
  (46 shorter events, 37.6 us)
Async XLA Ops:
  23.3 58.3 %all-to-all-start = ((f32[1,2,8,256,128]{4,2,1,0,3:T(8,128)}), f32[1,2,8,256,128]{4,2,1,0,3:T(8,128)}, u32[]{:S(2)}, u32[]{:S(2)}) async-start(f32[1,2,8,256,128]{4,2,1,0,3:T(8,128)} %copy.38), calls=%async_computation | async-start | bytes 4194304 | tf_op jit(solution)/shard_map/all_to_all | solution.py:72
  43.0 45.5 %copy-start.6 = (s32[2,3]{1,0:T(2,128)S(1)}, s32[2,3]{1,0:T(2,128)}, u32[]{:S(2)}) copy-start(s32[2,3]{1,0:T(2,128)} %param.5) | copy-start | bytes 76
  81.6 55.0 %all-to-all-start.2 = ((f32[1,2,8,256,128]{4,2,1,0,3:T(8,128)}), f32[1,2,8,256,128]{4,2,1,0,3:T(8,128)}, u32[]{:S(2)}, u32[]{:S(2)}) async-start(f32[1,2,8,256,128]{4,2,1,0,3:T(8,128)} %copy.50), calls=%async_computation.2 | async-start | bytes 4194304 | tf_op jit(solution)/shard_map/all_to_all | solution.py:72
  136.5 5.3 %copy-start.3 = (f32[1,2,256,8,128]{4,2,3,1,0:T(8,128)S(1)}, f32[1,2,256,8,128]{4,2,3,1,0:T(8,128)}, u32[]{:S(2)}) copy-start(f32[1,2,256,8,128]{4,2,3,1,0:T(8,128)} %fusion.41) | copy-start | bytes 6291460
  136.5 5.3 %copy-start.4 = (f32[1,256,8,128]{3,2,1,0:T(8,128)S(1)}, f32[1,256,8,128]{3,2,1,0:T(8,128)}, u32[]{:S(2)}) copy-start(f32[1,256,8,128]{3,2,1,0:T(8,128)} %get-tuple-element.26) | copy-start | bytes 3145732
  157.0 54.5 %all-to-all-start.1 = ((f32[1,2,256,8,128]{4,3,1,0,2:T(8,128)}), f32[1,2,256,8,128]{4,3,1,0,2:T(8,128)S(1)}, u32[]{:S(2)}, u32[]{:S(2)}) async-start(f32[1,2,256,8,128]{4,3,1,0,2:T(8,128)} %copy.43), calls=%async_computation.1 | async-start | bytes 4194304 | tf_op jit(solution)/shard_map/all_to_all | solution.py:75
  211.5 54.6 %all-to-all-start.3 = ((f32[1,2,256,8,128]{4,3,1,0,2:T(8,128)}), f32[1,2,256,8,128]{4,3,1,0,2:T(8,128)}, u32[]{:S(2)}, u32[]{:S(2)}) async-start(f32[1,2,256,8,128]{4,3,1,0,2:T(8,128)} %copy.54), calls=%async_computation.3 | async-start | bytes 4194304 | tf_op jit(solution)/shard_map/all_to_all | solution.py:75
  217.9 229.8 %all-reduce.3.cloned.1.call-start = ((), (), s32[]{:S(2)}) async-start(), calls=%async_computation.4 | async-start | bytes 6291456 | tf_op jit(solution)/shard_map/psum | solution.py:101
  266.1 5.3 %copy-start.2 = (f32[2,8,256,128]{3,2,1,0:T(8,128)S(1)}, f32[2,8,256,128]{3,2,1,0:T(8,128)}, u32[]{:S(2)}) copy-start(f32[2,8,256,128]{3,2,1,0:T(8,128)} %fusion.44) | copy-start | bytes 6291460
  273.4 2.2 copy-start
  447.7 1.9 copy-start.5
  452.8 3.4 copy-start.1
Sparse Core Ops, SparseCore 0:
  280.9 166.6 all-reduce.2
where the time goes:
time: 480 us; the launch traced here: 471 us
  waiting for transfers between devices  318 us (66%)
  matrix products  47.2 us (10%)
  local copies, waits for them, and re-layouts  32.2 us (7%)
  starting transfers between devices  29.9 us (6%)
  other arithmetic  29.7 us (6%)
  between operations  14.5 us (3%)
    psum x1, waiting for transfers between devices, shards(): numer_all, weight_all = lax.psum((numerator, weight), 'shot')  167 us
    all_to_all x2, waiting for transfers between devices, back_one(): lax.all_to_all(values, 'pencil', split_axis=2, concat_axis=3, tiled=True)  78.4 us
    all_to_all x2, waiting for transfers between devices, forward_one(): lax.all_to_all(values, 'pencil', split_axis=3, concat_axis=2, tiled=True)  72.6 us
    dot_general x4, matrix products, along_x(): jnp.einsum('scjyz,cdjk->sdkyz', values, matrix, precision=lax.Precision.H...  20.5 us
    dot_general x4, matrix products, along_y(): jnp.einsum('scxjz,cdjk->sdxkz', values, matrix, precision=lax.Precision.H...  17.4 us
    all_to_all x2, starting transfers between devices, forward_one(): lax.all_to_all(values, 'pencil', split_axis=3, concat_axis=2, tiled=True)  17.1 us
    unnamed x17, local copies, waits for them, and re-layouts  13 us
    all_to_all x2, starting transfers between devices, back_one(): lax.all_to_all(values, 'pencil', split_axis=2, concat_axis=3, tiled=True)  12.8 us
  transfers between devices with their start and end apart: 5, of which 5 were waited for; matrix products, arithmetic and copies ran while one was open for 9% of the time, Pallas kernels for 0%

commit v1 on v0

v1 whole, which is shorter than its diff:
```python
import functools
import math

import jax
import jax.numpy as jnp
import ml_dtypes
import numpy as np
from jax import lax
from jax.experimental import pallas as pl
from jax.experimental.pallas import tpu as pltpu
from jax.sharding import Mesh, PartitionSpec as P

SHOT = ("zh", "y")
PENCIL = ("zl", "x", "core")
ZH, YY = 2, 4
PARTS = 32
NX, NY, NZ = 256, 256, 128
PLANES = NX // PARTS
KY = NY // PARTS
SHARE = NY // (ZH * YY)
VMEM_LIMIT = 58 * 1024 * 1024


def split_table(table):
    high = table.astype(ml_dtypes.bfloat16)
    return high, (table - high.astype(np.float64)).astype(ml_dtypes.bfloat16)


def cos_sin(length):
    index = np.arange(length)
    angle = 2.0 * np.pi * (index[:, None] * index[None, :] % length) / length
    return np.cos(angle) / math.sqrt(length), np.sin(angle) / math.sqrt(length)


def long_table(order=None):
    cosine, sine = cos_sin(NY)
    if order is not None:
        cosine, sine = cosine[order], sine[order]
    high, low = split_table(np.concatenate([cosine, sine], axis=0))
    return np.concatenate([high, high, low], axis=1)


def z_table(sign):
    cosine, sine = cos_sin(NZ)
    high, low = split_table(np.block([[cosine, -sign * sine], [sign * sine, cosine]]))
    return np.concatenate([high, high, low], axis=0)


def three_terms(values, axis):
    high = values.astype(jnp.bfloat16)
    low = (values - high.astype(jnp.float32)).astype(jnp.bfloat16)
    return jnp.concatenate([high, low, high], axis=axis)


def dot(left, right):
    return lax.dot_general(left, right, (((1,), (0,)), ((), ())), preferred_element_type=jnp.float32)


def long_transform(table, values, sign):
    both = dot(table, three_terms(values, 0))
    count, lanes = both.shape[0] // 2, both.shape[1] // 2
    cos_re, cos_im = both[:count, :lanes], both[:count, lanes:]
    sin_re, sin_im = both[count:, :lanes], both[count:, lanes:]
    if sign > 0:
        return cos_re + sin_im, cos_im - sin_re
    return cos_re - sin_im, cos_im + sin_re


def table_spec(table):
    return pl.BlockSpec(table.shape, lambda *_: (0, 0))


def forward_kernel(member, cell_ref, w_ref, z_ref, y_ref, out_ref):
    plane = lax.axis_index(PENCIL) * PLANES + pl.program_id(0)
    real = w_ref[0, 0, 0]
    imag = w_ref[0, 1, 0]
    row = lax.broadcasted_iota(jnp.int32, (NY, NZ), 0)
    column = lax.broadcasted_iota(jnp.int32, (NY, NZ), 1)
    here = (row == cell_ref[member, 1]) & (column == cell_ref[member, 2])
    here = here & (plane == cell_ref[member, 0])
    real = real + jnp.where(here, math.sqrt(NX * NY * NZ), 0.0)
    values = jnp.concatenate([real, imag], axis=1)
    values = dot(three_terms(values, 1), z_ref[...])
    real, imag = long_transform(y_ref[...], values, 1)
    out_ref[:, 0, 0] = real.reshape(PARTS, KY, NZ)
    out_ref[:, 0, 1] = imag.reshape(PARTS, KY, NZ)


def forward(source, member, cells, z_dft, y_dft):
    return pl.pallas_call(
        functools.partial(forward_kernel, member),
        grid=(PLANES,),
        in_specs=[
            pl.BlockSpec(memory_space=pltpu.SMEM),
            pl.BlockSpec((1, 2, 1, NY, NZ), lambda i: (member, 0, i, 0, 0)),
            *[table_spec(t) for t in (z_dft, y_dft)],
        ],
        out_specs=pl.BlockSpec((PARTS, 1, 2, KY, NZ), lambda i: (0, i, 0, 0, 0)),
        out_shape=jax.ShapeDtypeStruct((PARTS, PLANES, 2, KY, NZ), jnp.float32),
        compiler_params=pltpu.CompilerParams(vmem_limit_bytes=VMEM_LIMIT),
        cost_estimate=pl.CostEstimate(flops=2400 * 10**6, bytes_accessed=4 * 2**20, transcendentals=0),
        name="forward_zy",
    )(cells, source, z_dft, y_dft)


def spectral_kernel(chunks, in_ref, green_ref, x_ref, back_ref, *refs):
    out_refs = [ref.reshape(PARTS * chunk * 2 * KY, NZ) for ref, chunk in zip(refs[-len(chunks) :], chunks)]

    def step(ky, carry):
        def take(c):
            return in_ref[pl.ds(c * KY + ky, NX, stride=2 * KY), :]

        values = jnp.concatenate([take(0), take(1)], axis=1)
        real, imag = long_transform(x_ref[...], values, 1)
        green_re = green_ref[pl.ds(ky, NX, stride=KY), :]
        green_im = green_ref[pl.ds(NX * KY + ky, NX, stride=KY), :]
        values = jnp.concatenate(
            [green_re * real - green_im * imag, green_re * imag + green_im * real], axis=1
        )
        results = long_transform(back_ref[...], values, -1)
        at = 0
        for chunk, out_ref in zip(chunks, out_refs):
            for plane in range(chunk):
                for c in range(2):
                    first = (plane * 2 + c) * KY + ky
                    rows = pl.ds(first, PARTS, stride=chunk * 2 * KY)
                    out_ref[rows, :] = results[c][at : at + PARTS]
                at += PARTS
        return carry

    lax.fori_loop(0, KY, step, 0)


def spectral(spectra, green, member, chunks, x_dft, back_dft, earlier):
    rows = 2 * KY * PARTS
    whole = [(rows * PLANES, NZ), (2 * NX * KY, NZ), *[t.shape for t in (x_dft, back_dft)]]
    return pl.pallas_call(
        functools.partial(spectral_kernel, chunks),
        grid=(1,),
        in_specs=[
            *[pl.BlockSpec(shape, lambda i: (0, 0)) for shape in whole],
            *[pl.BlockSpec(memory_space=pl.ANY) for _ in earlier],
        ],
        out_specs=[
            pl.BlockSpec((PARTS, 1, chunk, 2, KY, NZ), lambda i: (0, member, 0, 0, 0, 0))
            for chunk in chunks
        ],
        out_shape=[
            jax.ShapeDtypeStruct((PARTS, 2, chunk, 2, KY, NZ), jnp.float32) for chunk in chunks
        ],
        input_output_aliases={4 + i: i for i in range(len(earlier))},
        compiler_params=pltpu.CompilerParams(vmem_limit_bytes=VMEM_LIMIT),
        cost_estimate=pl.CostEstimate(flops=3200 * 10**6, bytes_accessed=6 * 2**20, transcendentals=0),
        name="spectral",
    )(
        spectra.reshape(rows * PLANES, NZ),
        green.reshape(2 * NX * KY, NZ),
        x_dft,
        back_dft,
        *earlier,
    )


def inverse_kernel(f_ref, w_ref, z_ref, y_ref, u_ref, sum_ref):
    here = lax.axis_index("y")
    total_re = total_im = weight = None
    for member in range(2):
        values = jnp.concatenate(
            [f_ref[:, member, 0, c].reshape(NY, NZ) for c in range(2)], axis=1
        )
        real, imag = long_transform(y_ref[...], values, -1)
        field = dot(three_terms(jnp.concatenate([real, imag], axis=1), 1), z_ref[...])
        real, imag = field[:, :NZ], field[:, NZ:]
        u_ref[member, 0, 0] = real
        u_ref[member, 1, 0] = imag
        source_re, source_im = w_ref[member, 0, 0], w_ref[member, 1, 0]
        term_re = real * source_re + imag * source_im
        term_im = real * source_im - imag * source_re
        term = real * real + imag * imag
        total_re = term_re if total_re is None else total_re + term_re
        total_im = term_im if total_im is None else total_im + term_im
        weight = term if weight is None else weight + term
    for kind, total in enumerate((total_re, total_im, weight)):
        total = total.reshape(ZH, YY, SHARE, NZ)
        for y in range(YY):
            sum_ref[lax.rem(y + YY - here, YY), :, kind, 0] = total[:, y]


def inverse(fields, sources, inside, start, count, z_dft, y_dft):
    return pl.pallas_call(
        inverse_kernel,
        grid=(count,),
        in_specs=[
            pl.BlockSpec((PARTS, 2, 1, 2, KY, NZ), lambda i: (0, 0, inside + i, 0, 0, 0)),
            pl.BlockSpec((2, 2, 1, NY, NZ), lambda i: (0, 0, start + i, 0, 0)),
            *[table_spec(t) for t in (z_dft, y_dft)],
        ],
        out_specs=[
            pl.BlockSpec((2, 2, 1, NY, NZ), lambda i: (0, 0, i, 0, 0)),
            pl.BlockSpec((YY, ZH, 3, 1, SHARE, NZ), lambda i: (0, 0, 0, i, 0, 0)),
        ],
        out_shape=[
            jax.ShapeDtypeStruct((2, 2, count, NY, NZ), jnp.float32),
            jax.ShapeDtypeStruct((YY, ZH, 3, count, SHARE, NZ), jnp.float32),
        ],
        compiler_params=pltpu.CompilerParams(vmem_limit_bytes=VMEM_LIMIT),
        cost_estimate=pl.CostEstimate(
            flops=600 * 10**6 * count, bytes_accessed=1900 * 1024 * count, transcendentals=0
        ),
        name="inverse_yz",
    )(fields, sources, z_dft, y_dft)


def update_kernel(*refs):
    parts, u_ref, w_ref, out_ref = refs[:YY], refs[YY], refs[YY + 1], refs[-1]
    here = lax.axis_index("y")
    for shift, part_ref in enumerate(parts):
        y = lax.rem(here + YY - shift, YY)
        for h in range(ZH):
            rows = pl.ds(pl.multiple_of((h * YY + y) * SHARE, SHARE), SHARE)
            real, imag = part_ref[h, 0, 0], part_ref[h, 1, 0]
            for member in range(2):
                field_re, field_im = u_ref[member, 0, 0, rows], u_ref[member, 1, 0, rows]
                scatter_re = real * field_re - imag * field_im
                scatter_im = real * field_im + imag * field_re
                out_ref[member, 0, 0, rows] = 0.5 * (w_ref[member, 0, 0, rows] + scatter_re)
                out_ref[member, 1, 0, rows] = 0.5 * (w_ref[member, 1, 0, rows] + scatter_im)


def update(parts, fields, sources, start, count, earlier):
    block = (2, 2, 1, NY, NZ)
    more = () if earlier is None else (earlier,)
    part_spec = pl.BlockSpec((ZH, 2, 1, SHARE, NZ), lambda i: (0, 0, i, 0, 0))
    return pl.pallas_call(
        update_kernel,
        grid=(count,),
        in_specs=[
            *[part_spec] * YY,
            pl.BlockSpec(block, lambda i: (0, 0, i, 0, 0)),
            pl.BlockSpec(block, lambda i: (0, 0, start + i, 0, 0)),
            *[pl.BlockSpec(memory_space=pl.ANY) for _ in more],
        ],
        out_specs=pl.BlockSpec(block, lambda i: (0, 0, start + i, 0, 0)),
        out_shape=jax.ShapeDtypeStruct(sources.shape, jnp.float32),
        input_output_aliases={YY + 2: 0} if more else {},
        compiler_params=pltpu.CompilerParams(vmem_limit_bytes=VMEM_LIMIT),
        cost_estimate=pl.CostEstimate(
            flops=10**6 * count, bytes_accessed=1800 * 1024 * count, transcendentals=0
        ),
        name="update",
    )(*parts, fields, sources, *more)


def exchange(values):
    return lax.all_to_all(values, PENCIL, split_axis=0, concat_axis=0, tiled=True)


def along_y(values, shift):
    return lax.ppermute(values, "y", [(i, (i + shift) % YY) for i in range(YY)])


def reduce_shots(sums):
    arrived = [along_y(sums[shift], shift) for shift in range(1, YY)]
    mine = sums[0] + arrived[0] + arrived[1] + arrived[2]
    both = mine + lax.ppermute(mine, "zh", [(0, 1), (1, 0)])
    return both[:, :2] / (1.0 + both[:, 2:])


def share_contrast(contrast):
    return [contrast, *[along_y(contrast, shift) for shift in range(1, YY)]]


CHUNKS = (4, 4)
PIECES = ((4,), (2, 2))


def shards(contrast_source, green_spectrum, source_cells):
    order = np.arange(NX).reshape(PARTS, PLANES).T.reshape(-1)
    y_dft = jnp.asarray(long_table())
    back_dft = jnp.asarray(long_table(order))
    z_forward = jnp.asarray(z_table(1))
    z_back = jnp.asarray(z_table(-1))

    images = []
    for member in range(2):
        spectra = exchange(forward(contrast_source, member, source_cells, z_forward, y_dft))
        images = spectral(spectra, green_spectrum, member, CHUNKS, y_dft, back_dft, images)
    updated = None
    shares = []
    start = 0
    parts = ()
    updates = []
    for image, pieces in zip(images, PIECES):
        fields, parts = lax.optimization_barrier((exchange(image), parts))
        inside = 0
        for count in pieces:
            field, sums = inverse(fields, contrast_source, inside, start, count, z_back, y_dft)
            contrast = reduce_shots(sums)
            shares.append(lax.dynamic_index_in_dim(contrast, lax.axis_index("zh"), 0, keepdims=False))
            parts = share_contrast(contrast)
            updates.append((parts, field, start, count))
            start += count
            inside += count
    for parts, field, start, count in updates:
        updated = update(parts, field, contrast_source, start, count, updated)
    return updated, jnp.concatenate(shares, axis=1)


def solution(mesh):
    fine = Mesh(mesh.devices.reshape(ZH, YY, 4, 4, 2), (*SHOT, *PENCIL))
    return jax.shard_map(
        shards,
        mesh=fine,
        in_specs=(
            P(SHOT, None, PENCIL, None, None),
            P(None, None, PENCIL, None),
            P(SHOT, None),
        ),
        out_specs=(P(SHOT, None, PENCIL, None, None), P(None, PENCIL, SHOT, None)),
        check_vma=False,
    )
```

time: 480 us -> 332 us (0.69)
  the two profiles are of different devices: /device:TPU:1 before, /device:TPU:38 now
where the time goes in v1:
time: 332 us; the launch traced here: 331 us
  waiting for transfers between devices  126 us (38%)
  Pallas kernels  76.5 us (23%)
  starting transfers between devices  65 us (20%)
  blocking collectives  55.8 us (17%)
  local copies, waits for them, and re-layouts  4.02 us (1%)
    all_to_all x3, waiting for transfers between devices, exchange(): lax.all_to_all(values, PENCIL, split_axis=0, concat_axis=0, tiled=True)  68 us
    all_to_all x1, blocking collectives, exchange(): lax.all_to_all(values, PENCIL, split_axis=0, concat_axis=0, tiled=True)  55.8 us
    ppermute x18, waiting for transfers between devices, along_y(): return lax.ppermute(values, 'y', [(i, (i + shift) % YY) for i in range(YY)])  32.7 us
    ppermute x18, starting transfers between devices, along_y(): return lax.ppermute(values, 'y', [(i, (i + shift) % YY) for i in range(YY)])  28.9 us
    pallas_call x2, Pallas kernels, spectral(): pl.pallas_call(functools.partial(spectral_kernel, chunks), grid=(1,), in_...  28.2 us
    ppermute x3, waiting for transfers between devices, reduce_shots(): both = mine + lax.ppermute(mine, 'zh', [(0, 1), (1, 0)])  24.8 us
    all_to_all x3, starting transfers between devices, exchange(): lax.all_to_all(values, PENCIL, split_axis=0, concat_axis=0, tiled=True)  24.7 us
    pallas_call x3, Pallas kernels, inverse(): pl.pallas_call(inverse_kernel, grid=(count,), in_specs=[pl.BlockSpec((PAR...  20 us
  transfers between devices with their start and end apart: 24, of which 11 were waited for; matrix products, arithmetic and copies ran while one was open for 2% of the time, Pallas kernels for 12%

profile of v1, /device:TPU:38, one launch (start us, length us, event | category | flops | bytes accessed | tf_op | source)
XLA Modules:
  0.0 331.0 jit_solution(8775034099487569440)
XLA Ops:
  0.6 9.3 %forward_zy.3 = f32[32,8,2,8,128]{4,3,2,1,0:T(8,128)} custom-call(s32[2,3]{1,0:T(2,128)} %cell_ref.3, f32[2,2,8,256,128]{4,3,2,1,0:T(8,128)} %refs_5_.5, bf16[768,256]{1,0:T(8,128)(2,1)} %constant.31.clone.z_ref, bf16[512,768]{1,0:T(8,128)(2,1)} %constant.29.clone.y_ref.x_ref), custom_call_target="tpu_custom_call" | custom-call | flops 2400000000 | bytes 4194304 | tf_op jit(solution)/shard_map/forward_zy/pallas_call | solution.py:90
  10.0 8.5 %all-to-all-start.1 = ((f32[32,8,2,8,128]{4,3,2,1,0:T(8,128)}), f32[32,8,2,8,128]{4,3,2,1,0:T(8,128)S(1)}, u32[]{:S(2)}, u32[]{:S(2)}) async-start(f32[32,8,2,8,128]{4,3,2,1,0:T(8,128)} %forward_zy.3), calls=%async_computation.1 | async-start | bytes 4194304 | tf_op jit(solution)/shard_map/all_to_all | solution.py:255
  18.5 9.3 %forward_zy.2 = f32[32,8,2,8,128]{4,3,2,1,0:T(8,128)} custom-call(s32[2,3]{1,0:T(2,128)} %cell_ref.3, f32[2,2,8,256,128]{4,3,2,1,0:T(8,128)} %refs_5_.5, bf16[768,256]{1,0:T(8,128)(2,1)} %constant.31.clone.z_ref, bf16[512,768]{1,0:T(8,128)(2,1)} %constant.29.clone.y_ref.x_ref), custom_call_target="tpu_custom_call" | custom-call | flops 2400000000 | bytes 4194304 | tf_op jit(solution)/shard_map/forward_zy/pallas_call | solution.py:90
  27.8 36.5 %all-to-all-done.1 = f32[32,8,2,8,128]{4,3,2,1,0:T(8,128)S(1)} async-done(((f32[32,8,2,8,128]{4,3,2,1,0:T(8,128)}), f32[32,8,2,8,128]{4,3,2,1,0:T(8,128)S(1)}, u32[]{:S(2)}, u32[]{:S(2)}) %all-to-all-start.1) | async-done | bytes 2097184 | tf_op jit(solution)/shard_map/all_to_all | solution.py:255
  64.3 8.8 %all-to-all-start = ((f32[32,8,2,8,128]{4,3,2,1,0:T(8,128)}), f32[32,8,2,8,128]{4,3,2,1,0:T(8,128)}, u32[]{:S(2)}, u32[]{:S(2)}) async-start(f32[32,8,2,8,128]{4,3,2,1,0:T(8,128)} %forward_zy.2), calls=%async_computation | async-start | bytes 4194304 | tf_op jit(solution)/shard_map/all_to_all | solution.py:255
  73.1 14.1 %spectral.2 = (f32[32,2,4,2,8,128]{5,4,3,2,1,0:T(8,128)}, f32[32,2,4,2,8,128]{5,4,3,2,1,0:T(8,128)}) custom-call(f32[4096,128]{1,0:T(8,128)} %bitcast.51, f32[4096,128]{1,0:T(8,128)} %bitcast.52, bf16[512,768]{1,0:T(8,128)(2,1)} %constant.29.clone.y_ref.x_ref, bf16[512,768]{1,0:T(8,128)(2,1)} %constant.30.clone.back_ref), custom_call_target="tpu_custom_call" | custom-call | flops 3200000000 | bytes 6291456 | tf_op jit(solution)/shard_map/spectral/pallas_call | solution.py:137
  87.2 31.6 %all-to-all-done = f32[32,8,2,8,128]{4,3,2,1,0:T(8,128)} async-done(((f32[32,8,2,8,128]{4,3,2,1,0:T(8,128)}), f32[32,8,2,8,128]{4,3,2,1,0:T(8,128)}, u32[]{:S(2)}, u32[]{:S(2)}) %all-to-all-start) | async-done | bytes 2097184 | tf_op jit(solution)/shard_map/all_to_all | solution.py:255
  118.8 14.1 %spectral.3 = (f32[32,2,4,2,8,128]{5,4,3,2,1,0:T(8,128)}, f32[32,2,4,2,8,128]{5,4,3,2,1,0:T(8,128)}) custom-call(f32[4096,128]{1,0:T(8,128)} %bitcast.in_ref, f32[4096,128]{1,0:T(8,128)} %bitcast.53, bf16[512,768]{1,0:T(8,128)(2,1)} %constant.29.clone.y_ref.x_ref, ...), custom_call_target="tpu_custom_call", output_to_operand_aliasing={{0}: (4, {}), {1}: (5, {})} | custom-call | flops 3200000000 | bytes 6291456 | tf_op jit(solution)/shard_map/spectral/pallas_call | solution.py:137
  132.8 55.8 %all_to_all.20.f_ref = f32[32,2,4,2,8,128]{5,4,3,2,1,0:T(8,128)} all-to-all(f32[32,2,4,2,8,128]{5,4,3,2,1,0:T(8,128)} %get-tuple-element.16), channel_id=1, replica_groups=mesh['zh'=2,'y'=4,'zl'=4,'x'=4,'core'=2] {'zl','x','core'}, dimensions={0} | all-to-all | bytes 4194304 | tf_op jit(solution)/shard_map/all_to_all | solution.py:255
  188.7 7.4 %all-to-all-start.2 = ((f32[32,2,4,2,8,128]{5,4,3,2,1,0:T(8,128)}), f32[32,2,4,2,8,128]{5,4,3,2,1,0:T(8,128)S(1)}, u32[]{:S(2)}, u32[]{:S(2)}) async-start(f32[32,2,4,2,8,128]{5,4,3,2,1,0:T(8,128)} %get-tuple-element.15), calls=%async_computation.2 | async-start | bytes 4194304 | tf_op jit(solution)/shard_map/all_to_all | solution.py:255
  196.1 8.6 %inverse_yz.3 = (f32[2,2,4,256,128]{4,3,2,1,0:T(8,128)}, f32[4,2,3,4,32,128]{5,4,3,2,1,0:T(8,128)}) custom-call(f32[32,2,4,2,8,128]{5,4,3,2,1,0:T(8,128)} %all_to_all.20.f_ref, f32[2,2,8,256,128]{4,3,2,1,0:T(8,128)} %refs_5_.5, bf16[768,256]{1,0:T(8,128)(2,1)} %constant.32.clone.z_ref, bf16[512,768]{1,0:T(8,128)(2,1)} %constant.29.clone.y_ref.x_ref), custom_call_target="tpu_custom_call" | custom-call | flops 2400000000 | bytes 7782400 | tf_op jit(solution)/shard_map/inverse_yz/pallas_call | solution.py:190
  211.9 6.6 %collective-permute-done = f32[2,3,4,32,128]{4,3,2,1,0:T(8,128)S(1)} collective-permute-done((f32[2,3,4,32,128]{4,3,2,1,0:T(8,128)S(1)}, f32[2,3,4,32,128]{4,3,2,1,0:T(8,128)S(1)}, u32[]{:S(2)}, u32[]{:S(2)}) %collective-permute-start) | collective-permute-done | bytes 393248 | tf_op jit(solution)/shard_map/ppermute | solution.py:259
  218.6 9.6 %collective-permute-done.1 = f32[2,3,4,32,128]{4,3,2,1,0:T(8,128)S(1)} collective-permute-done((f32[2,3,4,32,128]{4,3,2,1,0:T(8,128)S(1)}, f32[2,3,4,32,128]{4,3,2,1,0:T(8,128)S(1)}, u32[]{:S(2)}, u32[]{:S(2)}) %collective-permute-start.1) | collective-permute-done | bytes 393248 | tf_op jit(solution)/shard_map/ppermute | solution.py:259
  229.3 4.6 %collective-permute-start.3 = (f32[2,3,4,32,128]{4,3,2,1,0:T(8,128)S(1)}, f32[2,3,4,32,128]{4,3,2,1,0:T(8,128)S(1)}, u32[]{:S(2)}, u32[]{:S(2)}) collective-permute-start(f32[2,3,4,32,128]{4,3,2,1,0:T(8,128)S(1)} %fusion.1), channel_id=1, source_target_pairs={{0,128},{128,0},{1,129},{129,1},{2,130},{130,2},{3,131},{131,3},{4... | collective-permute-start | bytes 1179656 | tf_op jit(solution)/shard_map/ppermute | solution.py:265
  233.9 21.8 %collective-permute-done.3 = f32[2,3,4,32,128]{4,3,2,1,0:T(8,128)S(1)} collective-permute-done((f32[2,3,4,32,128]{4,3,2,1,0:T(8,128)S(1)}, f32[2,3,4,32,128]{4,3,2,1,0:T(8,128)S(1)}, u32[]{:S(2)}, u32[]{:S(2)}) %collective-permute-start.3) | collective-permute-done | bytes 393248 | tf_op jit(solution)/shard_map/ppermute | solution.py:265
  260.3 4.9 %collective-permute-done.4.refs_1_ = f32[2,2,4,32,128]{4,3,2,1,0:T(8,128)S(1)} collective-permute-done((f32[2,2,4,32,128]{4,3,2,1,0:T(8,128)S(1)}, f32[2,2,4,32,128]{4,3,2,1,0:T(8,128)S(1)}, u32[]{:S(2)}, u32[]{:S(2)}) %collective-permute-start.4) | collective-permute-done | bytes 262176 | tf_op jit(solution)/shard_map/ppermute | solution.py:259
  265.2 6.8 %collective-permute-done.5.refs_2_ = f32[2,2,4,32,128]{4,3,2,1,0:T(8,128)S(1)} collective-permute-done((f32[2,2,4,32,128]{4,3,2,1,0:T(8,128)S(1)}, f32[2,2,4,32,128]{4,3,2,1,0:T(8,128)S(1)}, u32[]{:S(2)}, u32[]{:S(2)}) %collective-permute-start.5) | collective-permute-done | bytes 262176 | tf_op jit(solution)/shard_map/ppermute | solution.py:259
  272.0 5.7 %inverse_yz.5 = (f32[2,2,2,256,128]{4,3,2,1,0:T(8,128)}, f32[4,2,3,2,32,128]{5,4,3,2,1,0:T(8,128)}) custom-call(f32[32,2,4,2,8,128]{5,4,3,2,1,0:T(8,128)} %copy-done, f32[2,2,8,256,128]{4,3,2,1,0:T(8,128)} %refs_5_.5, bf16[768,256]{1,0:T(8,128)(2,1)} %constant.32.clone.z_ref, bf16[512,768]{1,0:T(8,128)(2,1)} %constant.29.clone.y_ref.x_ref), custom_call_target="tpu_custom_call" | custom-call | flops 1200000000 | bytes 3891200 | tf_op jit(solution)/shard_map/inverse_yz/pallas_call | solution.py:190
  277.8 5.6 %inverse_yz.4 = (f32[2,2,2,256,128]{4,3,2,1,0:T(8,128)}, f32[4,2,3,2,32,128]{5,4,3,2,1,0:T(8,128)}) custom-call(f32[32,2,4,2,8,128]{5,4,3,2,1,0:T(8,128)} %copy-done, f32[2,2,8,256,128]{4,3,2,1,0:T(8,128)} %refs_5_.5, bf16[768,256]{1,0:T(8,128)(2,1)} %constant.32.clone.z_ref, bf16[512,768]{1,0:T(8,128)(2,1)} %constant.29.clone.y_ref.x_ref), custom_call_target="tpu_custom_call" | custom-call | flops 1200000000 | bytes 3891200 | tf_op jit(solution)/shard_map/inverse_yz/pallas_call | solution.py:190
  283.7 3.4 %collective-permute-start.15 = (f32[2,3,2,32,128]{4,3,2,1,0:T(8,128)S(1)}, f32[2,3,2,32,128]{4,3,2,1,0:T(8,128)S(1)}, u32[]{:S(2)}, u32[]{:S(2)}) collective-permute-start(f32[2,3,2,32,128]{4,3,2,1,0:T(8,128)S(1)} %get-tuple-element.29), channel_id=1, source_target_pairs={{0,64},{32,96},{64,0},{96,32},{1,65},{33,97},{65,1},{97,33},{2,66}... | collective-permute-start | bytes 589832 | tf_op jit(solution)/shard_map/ppermute | solution.py:259
  291.0 4.5 %update.3.refs_6_ = f32[2,2,8,256,128]{4,3,2,1,0:T(8,128)} custom-call(f32[2,2,4,32,128]{4,3,2,1,0:T(8,128)} %copy-done.2, f32[2,2,4,32,128]{4,3,2,1,0:T(8,128)} %copy-done.6, f32[2,2,4,32,128]{4,3,2,1,0:T(8,128)} %copy-done.7, f32[2,2,4,32,128]{4,3,2,1,0:T(8,128)} %copy-done.8, f32[2,2,4,256,128]{4,3,2,1,0:T(8,128)} %get-tuple-element.23.refs_4_, ...), custom_call_target="tpu_custom_call" | custom-call | flops 4000000 | bytes 7372800 | tf_op jit(solution)/shard_map/update/pallas_call | solution.py:234
  298.2 3.3 %collective-permute-start.17 = (f32[2,3,2,32,128]{4,3,2,1,0:T(8,128)S(1)}, f32[2,3,2,32,128]{4,3,2,1,0:T(8,128)S(1)}, u32[]{:S(2)}, u32[]{:S(2)}) collective-permute-start(f32[2,3,2,32,128]{4,3,2,1,0:T(8,128)S(1)} %fusion.3), channel_id=1, source_target_pairs={{0,128},{128,0},{1,129},{129,1},{2,130},{130,2},{3,131},{131,3},{4... | collective-permute-start | bytes 589832 | tf_op jit(solution)/shard_map/ppermute | solution.py:265
  305.5 3.4 %collective-permute-start.10 = (f32[2,3,2,32,128]{4,3,2,1,0:T(8,128)S(1)}, f32[2,3,2,32,128]{4,3,2,1,0:T(8,128)S(1)}, u32[]{:S(2)}, u32[]{:S(2)}) collective-permute-start(f32[2,3,2,32,128]{4,3,2,1,0:T(8,128)S(1)} %fusion.5), channel_id=1, source_target_pairs={{0,128},{128,0},{1,129},{129,1},{2,130},{130,2},{3,131},{131,3},{4... | collective-permute-start | bytes 589832 | tf_op jit(solution)/shard_map/ppermute | solution.py:265
  312.1 3.7 %collective-permute-start.19 = (f32[2,2,2,32,128]{4,3,2,1,0:T(8,128)S(1)}, f32[2,2,2,32,128]{4,3,2,1,0:T(8,128)S(1)}, u32[]{:S(2)}, u32[]{:S(2)}) collective-permute-start(f32[2,2,2,32,128]{4,3,2,1,0:T(8,128)S(1)} %slice_divide_fusion.1.refs_0_), channel_id=1, source_target_pairs={{0,64},{32,96},{64,0},{96,32},{1,65},{33,97},{65,1},{97,33},{2,66}... | collective-permute-start | bytes 393224 | tf_op jit(solution)/shard_map/ppermute | solution.py:259
  (84 shorter events, 42.1 us)
Async XLA Ops:
  10.0 54.3 %all-to-all-start.1 = ((f32[32,8,2,8,128]{4,3,2,1,0:T(8,128)}), f32[32,8,2,8,128]{4,3,2,1,0:T(8,128)S(1)}, u32[]{:S(2)}, u32[]{:S(2)}) async-start(f32[32,8,2,8,128]{4,3,2,1,0:T(8,128)} %forward_zy.3), calls=%async_computation.1 | async-start | bytes 4194304 | tf_op jit(solution)/shard_map/all_to_all | solution.py:255
  64.3 54.5 %all-to-all-start = ((f32[32,8,2,8,128]{4,3,2,1,0:T(8,128)}), f32[32,8,2,8,128]{4,3,2,1,0:T(8,128)}, u32[]{:S(2)}, u32[]{:S(2)}) async-start(f32[32,8,2,8,128]{4,3,2,1,0:T(8,128)} %forward_zy.2), calls=%async_computation | async-start | bytes 4194304 | tf_op jit(solution)/shard_map/all_to_all | solution.py:255
  188.7 71.7 %all-to-all-start.2 = ((f32[32,2,4,2,8,128]{5,4,3,2,1,0:T(8,128)}), f32[32,2,4,2,8,128]{5,4,3,2,1,0:T(8,128)S(1)}, u32[]{:S(2)}, u32[]{:S(2)}) async-start(f32[32,2,4,2,8,128]{5,4,3,2,1,0:T(8,128)} %get-tuple-element.15), calls=%async_computation.2 | async-start | bytes 4194304 | tf_op jit(solution)/shard_map/all_to_all | solution.py:255
  206.0 12.5 %collective-permute-start = (f32[2,3,4,32,128]{4,3,2,1,0:T(8,128)S(1)}, f32[2,3,4,32,128]{4,3,2,1,0:T(8,128)S(1)}, u32[]{:S(2)}, u32[]{:S(2)}) collective-permute-start(f32[2,3,4,32,128]{4,3,2,1,0:T(8,128)S(1)} %get-tuple-element.24), channel_id=1, source_target_pairs={{0,32},{32,64},{64,96},{96,0},{1,33},{33,65},{65,97},{97,1},{2,34}... | collective-permute-start | bytes 1179656 | tf_op jit(solution)/shard_map/ppermute | solution.py:259
  207.7 20.5 %collective-permute-start.1 = (f32[2,3,4,32,128]{4,3,2,1,0:T(8,128)S(1)}, f32[2,3,4,32,128]{4,3,2,1,0:T(8,128)S(1)}, u32[]{:S(2)}, u32[]{:S(2)}) collective-permute-start(f32[2,3,4,32,128]{4,3,2,1,0:T(8,128)S(1)} %get-tuple-element.26), channel_id=1, source_target_pairs={{0,64},{32,96},{64,0},{96,32},{1,65},{33,97},{65,1},{97,33},{2,66}... | collective-permute-start | bytes 1179656 | tf_op jit(solution)/shard_map/ppermute | solution.py:259
  210.6 17.6 %collective-permute-start.2 = (f32[2,3,4,32,128]{4,3,2,1,0:T(8,128)S(1)}, f32[2,3,4,32,128]{4,3,2,1,0:T(8,128)S(1)}, u32[]{:S(2)}, u32[]{:S(2)}) collective-permute-start(f32[2,3,4,32,128]{4,3,2,1,0:T(8,128)S(1)} %get-tuple-element.25), channel_id=1, source_target_pairs={{0,96},{32,0},{64,32},{96,64},{1,97},{33,1},{65,33},{97,65},{2,98}... | collective-permute-start | bytes 1179656 | tf_op jit(solution)/shard_map/ppermute | solution.py:259
  229.3 26.4 %collective-permute-start.3 = (f32[2,3,4,32,128]{4,3,2,1,0:T(8,128)S(1)}, f32[2,3,4,32,128]{4,3,2,1,0:T(8,128)S(1)}, u32[]{:S(2)}, u32[]{:S(2)}) collective-permute-start(f32[2,3,4,32,128]{4,3,2,1,0:T(8,128)S(1)} %fusion.1), channel_id=1, source_target_pairs={{0,128},{128,0},{1,129},{129,1},{2,130},{130,2},{3,131},{131,3},{4... | collective-permute-start | bytes 1179656 | tf_op jit(solution)/shard_map/ppermute | solution.py:265
  255.8 9.4 %collective-permute-start.4 = (f32[2,2,4,32,128]{4,3,2,1,0:T(8,128)S(1)}, f32[2,2,4,32,128]{4,3,2,1,0:T(8,128)S(1)}, u32[]{:S(2)}, u32[]{:S(2)}) collective-permute-start(f32[2,2,4,32,128]{4,3,2,1,0:T(8,128)S(1)} %slice_divide_fusion.refs_0_), channel_id=1, source_target_pairs={{0,32},{32,64},{64,96},{96,0},{1,33},{33,65},{65,97},{97,1},{2,34}... | collective-permute-start | bytes 786440 | tf_op jit(solution)/shard_map/ppermute | solution.py:259
  257.3 14.6 %collective-permute-start.5 = (f32[2,2,4,32,128]{4,3,2,1,0:T(8,128)S(1)}, f32[2,2,4,32,128]{4,3,2,1,0:T(8,128)S(1)}, u32[]{:S(2)}, u32[]{:S(2)}) collective-permute-start(f32[2,2,4,32,128]{4,3,2,1,0:T(8,128)S(1)} %slice_divide_fusion.refs_0_), channel_id=1, source_target_pairs={{0,64},{32,96},{64,0},{96,32},{1,65},{33,97},{65,1},{97,33},{2,66}... | collective-permute-start | bytes 786440 | tf_op jit(solution)/shard_map/ppermute | solution.py:259
  260.3 11.7 %collective-permute-start.6 = (f32[2,2,4,32,128]{4,3,2,1,0:T(8,128)S(1)}, f32[2,2,4,32,128]{4,3,2,1,0:T(8,128)S(1)}, u32[]{:S(2)}, u32[]{:S(2)}) collective-permute-start(f32[2,2,4,32,128]{4,3,2,1,0:T(8,128)S(1)} %slice_divide_fusion.refs_0_), channel_id=1, source_target_pairs={{0,96},{32,0},{64,32},{96,64},{1,97},{33,1},{65,33},{97,65},{2,98}... | collective-permute-start | bytes 786440 | tf_op jit(solution)/shard_map/ppermute | solution.py:259
  283.5 12.1 %collective-permute-start.14 = (f32[2,3,2,32,128]{4,3,2,1,0:T(8,128)S(1)}, f32[2,3,2,32,128]{4,3,2,1,0:T(8,128)S(1)}, u32[]{:S(2)}, u32[]{:S(2)}) collective-permute-start(f32[2,3,2,32,128]{4,3,2,1,0:T(8,128)S(1)} %get-tuple-element.27), channel_id=1, source_target_pairs={{0,32},{32,64},{64,96},{96,0},{1,33},{33,65},{65,97},{97,1},{2,34}... | collective-permute-start | bytes 589832 | tf_op jit(solution)/shard_map/ppermute | solution.py:259
  283.7 14.5 %collective-permute-start.15 = (f32[2,3,2,32,128]{4,3,2,1,0:T(8,128)S(1)}, f32[2,3,2,32,128]{4,3,2,1,0:T(8,128)S(1)}, u32[]{:S(2)}, u32[]{:S(2)}) collective-permute-start(f32[2,3,2,32,128]{4,3,2,1,0:T(8,128)S(1)} %get-tuple-element.29), channel_id=1, source_target_pairs={{0,64},{32,96},{64,0},{96,32},{1,65},{33,97},{65,1},{97,33},{2,66}... | collective-permute-start | bytes 589832 | tf_op jit(solution)/shard_map/ppermute | solution.py:259
  287.1 11.1 %collective-permute-start.16 = (f32[2,3,2,32,128]{4,3,2,1,0:T(8,128)S(1)}, f32[2,3,2,32,128]{4,3,2,1,0:T(8,128)S(1)}, u32[]{:S(2)}, u32[]{:S(2)}) collective-permute-start(f32[2,3,2,32,128]{4,3,2,1,0:T(8,128)S(1)} %get-tuple-element.28), channel_id=1, source_target_pairs={{0,96},{32,0},{64,32},{96,64},{1,97},{33,1},{65,33},{97,65},{2,98}... | collective-permute-start | bytes 589832 | tf_op jit(solution)/shard_map/ppermute | solution.py:259
  288.2 13.3 %collective-permute-start.7 = (f32[2,3,2,32,128]{4,3,2,1,0:T(8,128)S(1)}, f32[2,3,2,32,128]{4,3,2,1,0:T(8,128)S(1)}, u32[]{:S(2)}, u32[]{:S(2)}) collective-permute-start(f32[2,3,2,32,128]{4,3,2,1,0:T(8,128)S(1)} %get-tuple-element.30), channel_id=1, source_target_pairs={{0,32},{32,64},{64,96},{96,0},{1,33},{33,65},{65,97},{97,1},{2,34}... | collective-permute-start | bytes 589832 | tf_op jit(solution)/shard_map/ppermute | solution.py:259
  290.3 14.2 %collective-permute-start.8 = (f32[2,3,2,32,128]{4,3,2,1,0:T(8,128)S(1)}, f32[2,3,2,32,128]{4,3,2,1,0:T(8,128)S(1)}, u32[]{:S(2)}, u32[]{:S(2)}) collective-permute-start(f32[2,3,2,32,128]{4,3,2,1,0:T(8,128)S(1)} %get-tuple-element.32), channel_id=1, source_target_pairs={{0,64},{32,96},{64,0},{96,32},{1,65},{33,97},{65,1},{97,33},{2,66}... | collective-permute-start | bytes 589832 | tf_op jit(solution)/shard_map/ppermute | solution.py:259
  295.5 9.0 %collective-permute-start.9 = (f32[2,3,2,32,128]{4,3,2,1,0:T(8,128)S(1)}, f32[2,3,2,32,128]{4,3,2,1,0:T(8,128)S(1)}, u32[]{:S(2)}, u32[]{:S(2)}) collective-permute-start(f32[2,3,2,32,128]{4,3,2,1,0:T(8,128)S(1)} %get-tuple-element.31), channel_id=1, source_target_pairs={{0,96},{32,0},{64,32},{96,64},{1,97},{33,1},{65,33},{97,65},{2,98}... | collective-permute-start | bytes 589832 | tf_op jit(solution)/shard_map/ppermute | solution.py:259
  298.2 13.8 %collective-permute-start.17 = (f32[2,3,2,32,128]{4,3,2,1,0:T(8,128)S(1)}, f32[2,3,2,32,128]{4,3,2,1,0:T(8,128)S(1)}, u32[]{:S(2)}, u32[]{:S(2)}) collective-permute-start(f32[2,3,2,32,128]{4,3,2,1,0:T(8,128)S(1)} %fusion.3), channel_id=1, source_target_pairs={{0,128},{128,0},{1,129},{129,1},{2,130},{130,2},{3,131},{131,3},{4... | collective-permute-start | bytes 589832 | tf_op jit(solution)/shard_map/ppermute | solution.py:265
  305.5 11.9 %collective-permute-start.10 = (f32[2,3,2,32,128]{4,3,2,1,0:T(8,128)S(1)}, f32[2,3,2,32,128]{4,3,2,1,0:T(8,128)S(1)}, u32[]{:S(2)}, u32[]{:S(2)}) collective-permute-start(f32[2,3,2,32,128]{4,3,2,1,0:T(8,128)S(1)} %fusion.5), channel_id=1, source_target_pairs={{0,128},{128,0},{1,129},{129,1},{2,130},{130,2},{3,131},{131,3},{4... | collective-permute-start | bytes 589832 | tf_op jit(solution)/shard_map/ppermute | solution.py:265
  312.0 8.0 %collective-permute-start.18 = (f32[2,2,2,32,128]{4,3,2,1,0:T(8,128)S(1)}, f32[2,2,2,32,128]{4,3,2,1,0:T(8,128)S(1)}, u32[]{:S(2)}, u32[]{:S(2)}) collective-permute-start(f32[2,2,2,32,128]{4,3,2,1,0:T(8,128)S(1)} %slice_divide_fusion.1.refs_0_), channel_id=1, source_target_pairs={{0,32},{32,64},{64,96},{96,0},{1,33},{33,65},{65,97},{97,1},{2,34}... | collective-permute-start | bytes 393224 | tf_op jit(solution)/shard_map/ppermute | solution.py:259
  312.1 10.9 %collective-permute-start.19 = (f32[2,2,2,32,128]{4,3,2,1,0:T(8,128)S(1)}, f32[2,2,2,32,128]{4,3,2,1,0:T(8,128)S(1)}, u32[]{:S(2)}, u32[]{:S(2)}) collective-permute-start(f32[2,2,2,32,128]{4,3,2,1,0:T(8,128)S(1)} %slice_divide_fusion.1.refs_0_), channel_id=1, source_target_pairs={{0,64},{32,96},{64,0},{96,32},{1,65},{33,97},{65,1},{97,33},{2,66}... | collective-permute-start | bytes 393224 | tf_op jit(solution)/shard_map/ppermute | solution.py:259
  315.9 7.2 %collective-permute-start.20 = (f32[2,2,2,32,128]{4,3,2,1,0:T(8,128)S(1)}, f32[2,2,2,32,128]{4,3,2,1,0:T(8,128)S(1)}, u32[]{:S(2)}, u32[]{:S(2)}) collective-permute-start(f32[2,2,2,32,128]{4,3,2,1,0:T(8,128)S(1)} %slice_divide_fusion.1.refs_0_), channel_id=1, source_target_pairs={{0,96},{32,0},{64,32},{96,64},{1,97},{33,1},{65,33},{97,65},{2,98}... | collective-permute-start | bytes 393224 | tf_op jit(solution)/shard_map/ppermute | solution.py:259
  317.5 8.9 %collective-permute-start.11 = (f32[2,2,2,32,128]{4,3,2,1,0:T(8,128)S(1)}, f32[2,2,2,32,128]{4,3,2,1,0:T(8,128)S(1)}, u32[]{:S(2)}, u32[]{:S(2)}) collective-permute-start(f32[2,2,2,32,128]{4,3,2,1,0:T(8,128)S(1)} %slice_divide_fusion.2.refs_0_), channel_id=1, source_target_pairs={{0,32},{32,64},{64,96},{96,0},{1,33},{33,65},{65,97},{97,1},{2,34}... | collective-permute-start | bytes 393224 | tf_op jit(solution)/shard_map/ppermute | solution.py:259
  318.1 9.5 %collective-permute-start.12 = (f32[2,2,2,32,128]{4,3,2,1,0:T(8,128)S(1)}, f32[2,2,2,32,128]{4,3,2,1,0:T(8,128)S(1)}, u32[]{:S(2)}, u32[]{:S(2)}) collective-permute-start(f32[2,2,2,32,128]{4,3,2,1,0:T(8,128)S(1)} %slice_divide_fusion.2.refs_0_), channel_id=1, source_target_pairs={{0,64},{32,96},{64,0},{96,32},{1,65},{33,97},{65,1},{97,33},{2,66}... | collective-permute-start | bytes 393224 | tf_op jit(solution)/shard_map/ppermute | solution.py:259
  320.0 7.6 %collective-permute-start.13 = (f32[2,2,2,32,128]{4,3,2,1,0:T(8,128)S(1)}, f32[2,2,2,32,128]{4,3,2,1,0:T(8,128)S(1)}, u32[]{:S(2)}, u32[]{:S(2)}) collective-permute-start(f32[2,2,2,32,128]{4,3,2,1,0:T(8,128)S(1)} %slice_divide_fusion.2.refs_0_), channel_id=1, source_target_pairs={{0,96},{32,0},{64,32},{96,64},{1,97},{33,1},{65,33},{97,65},{2,98}... | collective-permute-start | bytes 393224 | tf_op jit(solution)/shard_map/ppermute | solution.py:259
  (15 other events, 98.9 us)
